TPU v7x, 256 devices: a whole 4x4x8 slice. The times are simulated.
256 devices in a mesh: ctx: 16 (over y, x), head: 8 (over z), pipe: 2 (over core).
Axes of the slice: x: 4, y: 4, z: 8, core: 2. Of those that a mesh axis runs over, the one named last changes fastest.
Arguments:
- queries: bfloat16 [2, 2048, 8192], P('pipe', 'ctx', 'head'), may hold values from -6 to 6
- keys: bfloat16 [2, 2048, 8192], P('pipe', 'ctx', 'head'), may hold values from -6 to 6
- values: bfloat16 [2, 2048, 8192], P('pipe', 'ctx', 'head'), may hold values from -6 to 6
- gates: bfloat16 [2, 2048, 8192], P('pipe', 'ctx', 'head'), may hold values from -6 to 6
- log_decay: float32 [2, 2048, 64], P('pipe', 'ctx', 'head'), may hold values from -1 to 0
- segment_ids: int32 [2, 2048], P('pipe', 'ctx'), may hold values from 0 to 7, never falling along the last dimension, each value on 1 to 512 neighbouring positions
- norm_gain: float32 [2, 8192], P('pipe', 'head'), may hold values from 0.1 to 1.9
- out_weight: bfloat16 [2, 8192, 6144], P('pipe', 'head', 'ctx'), may hold values from -0.0625 to 0.0625
Outputs:
- handed: bfloat16 [2, 2048, 6144], P('pipe', 'ctx', 'head')
Inputs may be any that keep to these rules, and one draw needn't show every extreme that they name: `segment_ids`: along each section's tokens the ids never fall; a document has at most a quarter of 2048 tokens, and one has exactly that many.
All inputs are finite; a program needn't handle non-finite values.
Results may differ from a plain program's by a relative error of at most 0.02.
Values may be sent and summed in bfloat16 or wider, within the bound.
A program may use at most 64 MiB of HBM per device.

v0:
```python
import jax
import jax.numpy as jnp
from jax import lax
from jax.sharding import PartitionSpec as P

DH = 128
highest = lax.Precision.HIGHEST


def entering(shard, axis, combine, identity):
    count, index = (lax.axis_size(axis), lax.axis_index(axis))
    everything = jax.tree.map(
        lambda part, kind: lax.all_gather(part.astype(kind), axis),
        shard,
        (jnp.bfloat16, jnp.bfloat16, jnp.bfloat16),
    )
    start = jax.tree.map(
        lambda part, zero: jnp.broadcast_to(jnp.asarray(zero, part.dtype), part.shape),
        shard,
        identity,
    )

    def hop(k, before):
        reached = k < index
        new = combine(
            before, jax.tree.map(lambda part, own: part[k].astype(own.dtype), everything, shard)
        )
        return jax.tree.map(lambda a, b: jnp.where(reached, a, b), new, before)

    return lax.fori_loop(0, count, hop, start)


def from_behind(shard, axis, by):
    count = lax.axis_size(axis)
    return lax.ppermute(shard, axis, [(i, (i + by) % count) for i in range(count)])


def block_step(carried, pieces):
    kv_state, doc_id = carried
    query_rows, key_rows, value_rows, rate_rows, doc_rows = pieces
    length = doc_rows.shape[0]
    running = jnp.cumsum(rate_rows, axis=0)
    running_t = running.T
    causal = lax.broadcasted_iota(jnp.int32, (length, length), 0) >= lax.broadcasted_iota(
        jnp.int32, (length, length), 1
    )
    allowed = causal & (doc_rows[:, None] == doc_rows[None, :])
    log_gaps = running_t[:, :, None] - running_t[:, None, :]
    weights = jnp.where(allowed[None], jnp.exp(jnp.where(allowed[None], log_gaps, 0.0)), 0.0)
    scores = jnp.einsum("ihd,jhd->hij", query_rows, key_rows, preferred_element_type=jnp.float32)
    mixed = (scores * weights).astype(jnp.bfloat16)
    inside = jnp.einsum("hij,jhd->ihd", mixed, value_rows, preferred_element_type=jnp.float32)
    value_full = value_rows.astype(jnp.float32)
    reaches = jnp.exp(running) * (doc_rows == doc_id).astype(jnp.float32)[:, None]
    carried_part = jnp.einsum(
        "ihd,hde->ihe",
        query_rows.astype(jnp.float32) * reaches[:, :, None],
        kv_state,
        precision=highest,
    )
    final_doc = doc_rows[-1]
    retain = (doc_id == final_doc).astype(jnp.float32)
    fading = (
        jnp.exp(running[-1][None, :] - running)
        * (doc_rows == final_doc).astype(jnp.float32)[:, None]
    )
    fresh_part = jnp.einsum(
        "jhd,jhe->hde",
        key_rows.astype(jnp.float32) * fading[:, :, None],
        value_full,
        precision=highest,
    )
    new_state = retain * jnp.exp(running[-1])[:, None, None] * kv_state + fresh_part
    return ((new_state, final_doc), inside + carried_part)


def sweep(query3, key3, value3, rate_rows, doc_rows, start_state, start_doc):
    rows_here = doc_rows.shape[0]
    heads_here = query3.shape[1]
    block_len = min(512, rows_here)
    block_count = rows_here // block_len
    pieces = (
        query3.reshape(block_count, block_len, heads_here, DH),
        key3.reshape(block_count, block_len, heads_here, DH),
        value3.reshape(block_count, block_len, heads_here, DH),
        rate_rows.reshape(block_count, block_len, heads_here),
        doc_rows.reshape(block_count, block_len),
    )
    final_carry, attended = lax.scan(block_step, (start_state, start_doc), pieces)
    return (final_carry[0], attended.reshape(rows_here, heads_here, DH))


def combine_pair(earlier, later):
    rate_early, state_early, doc_early = earlier
    rate_late, state_late, doc_late = later
    linked = ((doc_early == doc_late) | (doc_early < 0) | (doc_late < 0)).astype(jnp.float32)
    merged = linked[0] * rate_late[:, None, None] * state_early + state_late
    return (rate_early * rate_late, merged, jnp.where(doc_late < 0, doc_early, doc_late))


def carry_in(shard_rates, shard_state, shard_doc):
    heads_here = shard_rates.shape[0]
    neutral = (
        jnp.ones((heads_here,), jnp.float32),
        jnp.zeros((heads_here, DH, DH), jnp.float32),
        jnp.full((1,), -1.0, jnp.float32),
    )
    prefix = entering((shard_rates, shard_state, shard_doc), "ctx", combine_pair, neutral)
    return (prefix[1], prefix[2])


def on_device(queries, keys, values, gates, log_decay, segment_ids, norm_gain, out_weight):
    rows_here = queries.shape[1]
    width = queries.shape[2]
    heads_here = width // DH
    query3 = queries[0].reshape(rows_here, heads_here, DH)
    key3 = keys[0].reshape(rows_here, heads_here, DH)
    value3 = values[0].reshape(rows_here, heads_here, DH)
    rate_rows = log_decay[0]
    doc_rows = segment_ids[0].astype(jnp.float32)
    running = jnp.cumsum(rate_rows, axis=0)
    shard_rates = jnp.exp(running[-1])
    shard_doc = doc_rows[-1:]
    fading = (
        jnp.exp(running[-1][None, :] - running)
        * (doc_rows == shard_doc[0]).astype(jnp.float32)[:, None]
    )
    shard_state = jnp.einsum(
        "jhd,jhe->hde",
        key3.astype(jnp.float32) * fading[:, :, None],
        value3.astype(jnp.float32),
        precision=highest,
    )
    incoming, incoming_doc = carry_in(shard_rates, shard_state, shard_doc)
    ignored, attended = sweep(query3, key3, value3, rate_rows, doc_rows, incoming, incoming_doc[0])
    scaling = lax.rsqrt(jnp.mean(attended * attended, axis=-1, keepdims=True) + 1e-06)
    normed = (
        (attended * scaling).reshape(rows_here, width)
        * norm_gain[0][None, :]
        * jax.nn.sigmoid(gates[0].astype(jnp.float32))
    ).astype(jnp.bfloat16)
    weight_here = out_weight[0]
    partial_value = jnp.dot(
        normed,
        lax.all_gather(weight_here, "ctx", axis=1, tiled=True),
        preferred_element_type=jnp.float32,
    )
    summed = lax.psum_scatter(
        partial_value.astype(jnp.bfloat16), "head", scatter_dimension=1, tiled=True
    )
    handed = from_behind(summed, "pipe", 1)
    return handed[None]


def solution(mesh):
    return jax.shard_map(
        on_device,
        mesh=mesh,
        in_specs=(
            P("pipe", "ctx", "head"),
            P("pipe", "ctx", "head"),
            P("pipe", "ctx", "head"),
            P("pipe", "ctx", "head"),
            P("pipe", "ctx", "head"),
            P("pipe", "ctx"),
            P("pipe", "head"),
            P("pipe", "head", "ctx"),
        ),
        out_specs=P("pipe", "ctx", "head"),
        check_vma=False,
    )
```

profile of v0, /device:TPU:1, one launch (start us, length us, event | category | flops | bytes accessed | tf_op | source)
XLA Modules:
  0.0 237.9 jit_solution(17835527506379368174)
XLA Ops:
  6.5 0.8 copy.22
  8.8 1.3 compare_convert_fusion.1
  10.2 1.1 copy.36
  11.3 1.0 copy.39
  12.3 1.1 convolution_convert_fusion
  13.5 0.7 all-gather.8.cloned.1.call-update
  15.0 1.3 dynamic-slice.1
  16.2 0.8 dynamic-update-slice
  17.0 34.4 %all-reduce = bf16[16]{0:T(256)(128)(2,1)S(1)} all-reduce(bf16[16]{0:T(256)(128)(2,1)S(1)} %dynamic-update-slice), channel_id=1, replica_groups=mesh['ctx'=16,'head'=8,'pipe'=2] {'ctx'}, use_global_device_ids=true, to_apply=%add | all-reduce | flops 16 | bytes 64
  51.4 14.6 %all-gather.2 = bf16[16,1,8]{2,1,0:T(2,128)(2,1)S(1)} all-gather(bf16[1,1,8]{2,1,0:T(2,128)(2,1)S(1)} %get-tuple-element.212), channel_id=1, replica_groups=mesh['ctx'=16,'head'=8,'pipe'=2] {'ctx'}, dimensions={0}, use_global_device_ids=true | all-gather | bytes 272 | tf_op jit(solution)/shard_map/all_gather | solution.py:13
  65.9 1.0 copy.38
  67.1 7.1 %all-gather.6.cloned.1.call-done = bf16[128,128,128]{2,1,0:T(8,128)(2,1)} async-done(((bf16[8,128,128]{2,1,0:T(8,128)(2,1)}), bf16[128,128,128]{2,1,0:T(8,128)(2,1)}) %all-gather.6.cloned.1.call-update) | async-done | bytes 4194320 | tf_op jit(solution)/shard_map/all_gather | solution.py:13
  74.2 62.4 %while.10 = (s32[]{:T(128)}, f32[8,128,128]{2,1,0:T(8,128)S(1)}, f32[1]{0:T(128)}, s32[]{:T(128)}, bf16[16,1]{0,1:T(2,128)(2,1)S(1)}, /*index=5*/bf16[16,8]{1,0:...) while((s32[]{:T(128)}, f32[8,128,128]{2,1,0:T(8,128)S(1)}, ...), condition=%wide.region_2.3_spmd.clone, body=%wide.region_1.2_spmd.clone.sunk | while | flops 655388 | bytes 1310999 | solution.py:30
  76.3 1.1 fusion.44
  78.1 0.7 constant_dynamic-slice_fusion.3
  80.2 1.1 fusion.44
  82.0 0.7 constant_dynamic-slice_fusion.3
  84.1 1.1 fusion.44
  85.9 0.7 constant_dynamic-slice_fusion.3
  88.0 1.1 fusion.44
  89.8 0.7 constant_dynamic-slice_fusion.3
  91.9 1.1 fusion.44
  93.7 0.7 constant_dynamic-slice_fusion.3
  95.8 1.1 fusion.44
  97.6 0.7 constant_dynamic-slice_fusion.3
  99.7 1.1 fusion.44
  101.5 0.7 constant_dynamic-slice_fusion.3
  103.6 1.1 fusion.44
  105.4 0.7 constant_dynamic-slice_fusion.3
  107.5 1.1 fusion.44
  109.3 0.7 constant_dynamic-slice_fusion.3
  111.4 1.1 fusion.44
  113.2 0.7 constant_dynamic-slice_fusion.3
  115.3 1.1 fusion.44
  117.1 0.7 constant_dynamic-slice_fusion.3
  119.2 1.1 fusion.44
  121.0 0.7 constant_dynamic-slice_fusion.3
  123.1 1.1 fusion.44
  127.0 1.1 fusion.44
  130.9 1.1 fusion.44
  134.8 1.1 fusion.44
  136.8 1.3 convolution_bitcast_fusion.1
  138.9 41.3 %all-gather.8.cloned.1.call-done = bf16[1,1024,6144]{2,1,0:T(8,128)(2,1)} async-done(((bf16[1,1024,384]{2,1,0:T(8,128)(2,1)}), bf16[1,1024,6144]{2,1,0:T(8,128)(2,1)}) %all-gather.8.cloned.1.call-update) | async-done | bytes 12582928 | tf_op jit(solution)/shard_map/all_gather | solution.py:145
  180.1 7.6 %fusion.6 = bf16[128,6144]{1,0:T(8,128)(2,1)} fusion(bf16[1,1024,6144]{2,1,0:T(8,128)(2,1)} %all-gather.8.cloned.1.call-done, bf16[1,128,1024]{2,1,0:T(8,128)(2,1)S(1)} %copy-done, f32[128,1024]{1,0:T(8,128)S(1)} %copy.34, f32[1024]{0:T(1024)S(1)} %bitcast.81), kind=kOutput, calls=%fused_computation.9 | convolution fusion | flops 1612316672 | bytes 14946304 | tf_op jit(solution)/shard_map/dot_general | solution.py:143
  187.8 37.0 %reduce-scatter.2.cloned.1.call-done = bf16[128,768]{1,0:T(8,128)(2,1)} async-done(((bf16[128,6144]{1,0:T(8,128)(2,1)}), bf16[128,768]{1,0:T(8,128)(2,1)}) %reduce-scatter.2.cloned.1.call-update) | async-done | bytes 196624 | tf_op jit(solution)/shard_map/reduce_scatter | solution.py:148
  224.8 4.6 %collective-permute-start = (bf16[128,768]{1,0:T(8,128)(2,1)}, bf16[128,768]{1,0:T(8,128)(2,1)S(1)}, u32[]{:S(2)}, u32[]{:S(2)}) collective-permute-start(bf16[128,768]{1,0:T(8,128)(2,1)} %reduce-scatter.2.cloned.1.call-done), channel_id=1, source_target_pairs={{0,1},{1,0},{2,3},{3,2},{4,5},{5,4},{6,7},{7,6},{8,9},{9,8},{10,11... | collective-permute-start | bytes 589832 | tf_op jit(solution)/shard_map/ppermute | solution.py:35
  229.4 1.3 collective-permute-done
  230.7 0.7 copy.70
  (49 shorter events, 5.6 us)
Async XLA Ops:
  6.5 67.7 %all-gather.6.cloned.1.call-start = ((), (), s32[]{:S(2)}) async-start(), calls=%async_computation.2 | async-start | bytes 4456448 | tf_op jit(solution)/shard_map/all_gather | solution.py:13
  13.5 123.2 %copy-start.2 = (s32[1,128]{1,0:T(1,128)S(1)}, s32[1,128]{1,0:T(1,128)}, u32[]{:S(2)}) copy-start(s32[1,128]{1,0:T(1,128)} %param.15) | copy-start | bytes 1540
  13.5 166.6 %all-gather.8.cloned.1.call-start = ((), (), s32[]{:S(2)}) async-start(), calls=%async_computation.3 | async-start | bytes 13369344 | tf_op jit(solution)/shard_map/all_gather | solution.py:145
  14.2 210.5 %reduce-scatter.2.cloned.1.call-start = ((), (), s32[]{:S(2)}) async-start(), calls=%async_computation.1 | async-start | bytes 1769472 | tf_op jit(solution)/shard_map/reduce_scatter | solution.py:148
  136.6 43.5 %copy-start = (bf16[1,128,1024]{2,1,0:T(8,128)(2,1)S(1)}, bf16[1,128,1024]{2,1,0:T(8,128)(2,1)}, u32[]{:S(2)}) copy-start(bf16[1,128,1024]{2,1,0:T(8,128)(2,1)} %param.13) | copy-start | bytes 786436
  136.6 43.5 %copy-start.1 = (f32[1,1024]{1,0:T(1,128)S(1)}, f32[1,1024]{1,0:T(1,128)}, u32[]{:S(2)}) copy-start(f32[1,1024]{1,0:T(1,128)} %param.16) | copy-start | bytes 12292
  224.8 5.9 %collective-permute-start = (bf16[128,768]{1,0:T(8,128)(2,1)}, bf16[128,768]{1,0:T(8,128)(2,1)S(1)}, u32[]{:S(2)}, u32[]{:S(2)}) collective-permute-start(bf16[128,768]{1,0:T(8,128)(2,1)} %reduce-scatter.2.cloned.1.call-done), channel_id=1, source_target_pairs={{0,1},{1,0},{2,3},{3,2},{4,5},{5,4},{6,7},{7,6},{8,9},{9,8},{10,11... | collective-permute-start | bytes 589832 | tf_op jit(solution)/shard_map/ppermute | solution.py:35
Sparse Core Ops, SparseCore 0:
  13.6 60.5 all-gather.5
  76.6 103.4 all-gather.7
  187.9 36.8 reduce-scatter.1
where the time goes:
time: 239 us; the launch traced here: 238 us
  waiting for transfers between devices  87.4 us (37%)
  blocking collectives  48.9 us (20%)
  loops' own time  34.1 us (14%)
  other arithmetic  20.2 us (8%)
  local copies, waits for them, and re-layouts  18.2 us (8%)
  between operations  13.9 us (6%)
  matrix products  10.5 us (4%)
  starting transfers between devices  4.7 us (2%)
    all_gather x1, waiting for transfers between devices, on_device(): lax.all_gather(weight_here, 'ctx', axis=1, tiled=True)  41.3 us
    reduce_scatter x1, waiting for transfers between devices, on_device(): lax.psum_scatter(partial_value.astype(jnp.bfloat16), 'head', scatter_dime...  37 us
    unnamed x1, blocking collectives  34.4 us
    another operation x1, loops' own time, entering(): return lax.fori_loop(0, count, hop, start)  34.1 us
    select_n x16, other arithmetic, hop(): return jax.tree.map(lambda a, b: jnp.where(reached, a, b), new, before)  17.5 us
    all_gather x1, blocking collectives, entering(): lax.all_gather(part.astype(kind), axis)  14.6 us
    dynamic_slice x16, local copies, waits for them, and re-layouts, hop(): part[k].astype(own.dtype)  10.6 us
    dot_general x1, matrix products, on_device(): jnp.dot(normed, lax.all_gather(weight_here, 'ctx', axis=1, tiled=True), p...  7.63 us
  transfers between devices with their start and end apart: 4, of which 4 were waited for; matrix products, arithmetic and copies ran while one was open for 14% of the time, Pallas kernels for 0%

commit v1 on v0

--- a/solution.py
+++ b/solution.py
@@ -142,7 +142,9 @@
     weight_here = out_weight[0]
     partial_value = jnp.dot(
         normed,
-        lax.all_gather(weight_here, "ctx", axis=1, tiled=True),
+        jnp.concatenate(
+            lax.all_to_all(jnp.stack([weight_here] * lax.axis_size("ctx")), "ctx", 0, 0), axis=1
+        ),
         preferred_element_type=jnp.float32,
     )
     summed = lax.psum_scatter(

time: 239 us -> 406 us (1.70)
  blocking collectives: 48.9 us -> 241 us
  waiting for transfers between devices: 87.4 us -> 54.6 us
  starting transfers between devices: 4.7 us -> 12.4 us
  loops' own time: 34.1 us -> 27.4 us
  local copies, waits for them, and re-layouts: 18.2 us -> 22.4 us
    unnamed x1, blocking collectives: 34.4 us -> 228 us
    all_gather x1 -> x0, waiting for transfers between devices: 41.3 us -> none  [on_device(): lax.all_gather(weight_here, 'ctx', axis=1, tiled=True)]
    reduce_scatter x1, waiting for transfers between devices: 37 us -> 53.2 us  [on_device(): lax.psum_scatter(partial_value.astype(jnp.bfloat16), 'head', scatter_dime...]
    all_to_all x0 -> x1, starting transfers between devices: none -> 7.77 us  [on_device(): lax.all_to_all(jnp.stack([weight_here] * lax.axis_size('ctx')), 'ctx', 0, 0)]
    another operation x0 -> x2, local copies, waits for them, and re-layouts: none -> 7.54 us  [the longest x1 6.14 us: on_device(): jnp.stack([weight_here] * lax.axis_size('ctx'))]
    all_gather x1, waiting for transfers between devices: 7.12 us -> 0.02 us  [entering(): lax.all_gather(part.astype(kind), axis)]
    another operation x1, loops' own time: 34.1 us -> 27.4 us  [entering(): return lax.fori_loop(0, count, hop, start)]
  transfers between devices with their start and end apart: 4 -> 4, of which waited for: 4 -> 2; matrix products, arithmetic and copies ran while one was open for 14% -> 9% of each run, Pallas kernels for 0% -> 0%
where the time goes in v1:
time: 406 us; the launch traced here: 405 us
  blocking collectives  241 us (59%)
  waiting for transfers between devices  54.6 us (13%)
  loops' own time  27.4 us (7%)
  local copies, waits for them, and re-layouts  22.4 us (6%)
  other arithmetic  20.5 us (5%)
  between operations  14.2 us (3%)
  matrix products  12.9 us (3%)
  starting transfers between devices  12.4 us (3%)
    unnamed x1, blocking collectives  228 us
    reduce_scatter x1, waiting for transfers between devices, on_device(): lax.psum_scatter(partial_value.astype(jnp.bfloat16), 'head', scatter_dime...  53.2 us
    another operation x1, loops' own time, entering(): return lax.fori_loop(0, count, hop, start)  27.4 us
    select_n x16, other arithmetic, hop(): return jax.tree.map(lambda a, b: jnp.where(reached, a, b), new, before)  17.5 us
    all_gather x1, blocking collectives, entering(): lax.all_gather(part.astype(kind), axis)  13 us
    dot_general x1, matrix products, on_device(): jnp.dot(normed, jnp.concatenate(lax.all_to_all(jnp.stack([weight_here] *...  10 us
    dynamic_slice x16, local copies, waits for them, and re-layouts, hop(): part[k].astype(own.dtype)  8.93 us
  transfers between devices with their start and end apart: 4, of which 2 were waited for; matrix products, arithmetic and copies ran while one was open for 9% of the time, Pallas kernels for 0%

profile of v1, /device:TPU:1, one launch (start us, length us, event | category | flops | bytes accessed | tf_op | source)
XLA Modules:
  0.0 405.1 jit_solution(7000052862834203248)
XLA Ops:
  6.5 0.7 convert_bitcast_fusion.1
  7.2 0.6 slice.13
  7.8 1.3 compare_convert_fusion.1
  9.1 0.8 copy.38
  10.2 1.1 copy.54
  11.3 1.0 copy.56
  12.3 1.1 convolution_convert_fusion.1
  13.5 1.4 copy.51
  14.9 6.1 %stack.3 = bf16[16,1024,384]{1,2,0:T(8,128)(2,1)} broadcast(bf16[1024,384]{0,1:T(8,128)(2,1)S(1)} %copy.51), dimensions={1,2} | broadcast | bytes 13369344 | tf_op jit(solution)/shard_map/stack | solution.py:146
  21.1 7.8 %all-to-all-start = ((bf16[16,1024,384]{1,2,0:T(8,128)(2,1)}), bf16[16,1024,384]{1,2,0:T(8,128)(2,1)}, u32[]{:S(2)}, u32[]{:S(2)}) async-start(bf16[16,1024,384]{1,2,0:T(8,128)(2,1)} %stack.3), calls=%async_computation | async-start | bytes 25165824 | tf_op jit(solution)/shard_map/all_to_all | solution.py:146
  29.6 0.6 dynamic-slice.1
  30.2 0.8 dynamic-update-slice
  30.9 227.6 %all-reduce = bf16[16]{0:T(256)(128)(2,1)S(1)} all-reduce(bf16[16]{0:T(256)(128)(2,1)S(1)} %dynamic-update-slice), channel_id=1, replica_groups=mesh['ctx'=16,'head'=8,'pipe'=2] {'ctx'}, use_global_device_ids=true, to_apply=%add | all-reduce | flops 16 | bytes 64
  258.5 13.0 %all-gather.1 = bf16[16,1,8]{2,1,0:T(2,128)(2,1)S(1)} all-gather(bf16[1,1,8]{2,1,0:T(2,128)(2,1)S(1)} %get-tuple-element.219), channel_id=1, replica_groups=mesh['ctx'=16,'head'=8,'pipe'=2] {'ctx'}, dimensions={0}, use_global_device_ids=true | all-gather | bytes 272 | tf_op jit(solution)/shard_map/all_gather | solution.py:13
  272.1 54.1 %while.10 = (s32[]{:T(128)}, f32[8,128,128]{2,1,0:T(8,128)S(1)}, f32[1]{0:T(128)}, s32[]{:T(128)}, bf16[16,1]{0,1:T(2,128)(2,1)S(1)}, /*index=5*/bf16[16,8]{1,0:...) while((s32[]{:T(128)}, f32[8,128,128]{2,1,0:T(8,128)S(1)}, ...), condition=%wide.region_2.3_spmd.clone, body=%wide.region_1.2_spmd.clone.sunk | while | flops 655388 | bytes 1311015 | solution.py:30
  272.1 0.6 constant_dynamic-slice_fusion.3
  274.3 1.1 fusion.36
  275.5 0.6 constant_dynamic-slice_fusion.3
  277.7 1.1 fusion.36
  278.9 0.6 constant_dynamic-slice_fusion.3
  281.1 1.1 fusion.36
  282.2 0.6 constant_dynamic-slice_fusion.3
  284.5 1.1 fusion.36
  285.6 0.6 constant_dynamic-slice_fusion.3
  287.9 1.1 fusion.36
  289.0 0.6 constant_dynamic-slice_fusion.3
  291.2 1.1 fusion.36
  292.4 0.6 constant_dynamic-slice_fusion.3
  294.6 1.1 fusion.36
  295.8 0.6 constant_dynamic-slice_fusion.3
  298.0 1.1 fusion.36
  299.1 0.6 constant_dynamic-slice_fusion.3
  301.4 1.1 fusion.36
  302.5 0.6 constant_dynamic-slice_fusion.3
  304.8 1.1 fusion.36
  305.9 0.6 constant_dynamic-slice_fusion.3
  308.2 1.1 fusion.36
  311.5 1.1 fusion.36
  314.9 1.1 fusion.36
  318.3 1.1 fusion.36
  321.7 1.1 fusion.36
  325.1 1.1 fusion.36
  326.3 1.3 convolution_bitcast_fusion.1
  328.3 10.0 %convolution_convert_fusion = bf16[128,6144]{1,0:T(8,128)(2,1)} fusion(bf16[128,1024]{0,1:T(8,128)(2,1)S(1)} %bitcast.65, bf16[1024,6144]{0,1:T(8,128)(2,1)} %bitcast.20), kind=kOutput, calls=%fused_computation.7 | convolution fusion | flops 1611399168 | bytes 14417920 | tf_op jit(solution)/shard_map/dot_general | solution.py:143
  338.4 53.2 %reduce-scatter.2.cloned.1.call-done = bf16[128,768]{1,0:T(8,128)(2,1)} async-done(((bf16[128,6144]{1,0:T(8,128)(2,1)}), bf16[128,768]{1,0:T(8,128)(2,1)}) %reduce-scatter.2.cloned.1.call-update) | async-done | bytes 196624 | tf_op jit(solution)/shard_map/reduce_scatter | solution.py:150
  391.7 4.6 %collective-permute-start = (bf16[128,768]{1,0:T(8,128)(2,1)}, bf16[128,768]{1,0:T(8,128)(2,1)S(1)}, u32[]{:S(2)}, u32[]{:S(2)}) collective-permute-start(bf16[128,768]{1,0:T(8,128)(2,1)} %reduce-scatter.2.cloned.1.call-done), channel_id=1, source_target_pairs={{0,1},{1,0},{2,3},{3,2},{4,5},{5,4},{6,7},{7,6},{8,9},{9,8},{10,11... | collective-permute-start | bytes 589832 | tf_op jit(solution)/shard_map/ppermute | solution.py:35
  396.3 1.3 collective-permute-done
  397.5 0.7 copy.87
  (55 shorter events, 4.8 us)
Async XLA Ops:
  6.5 265.5 %all-gather.4.cloned.1.call-start = ((), (), s32[]{:S(2)}) async-start(), calls=%async_computation.3 | async-start | bytes 4456448 | tf_op jit(solution)/shard_map/all_gather | solution.py:13
  21.0 8.5 %copy-start.4 = (u32[256]{0:T(256)S(1)}, u32[256]{0:T(256)}, u32[]{:S(2)}) copy-start(u32[256]{0:T(256)} %constant.78) | copy-start | bytes 3076
  21.0 250.5 %copy-start.1 = (bf16[1,128,1024]{2,1,0:T(8,128)(2,1)S(1)}, bf16[1,128,1024]{2,1,0:T(8,128)(2,1)}, u32[]{:S(2)}) copy-start(bf16[1,128,1024]{2,1,0:T(8,128)(2,1)} %param.10) | copy-start | bytes 786436
  21.0 250.5 %copy-start = (bf16[1,128,1024]{2,1,0:T(8,128)(2,1)S(1)}, bf16[1,128,1024]{2,1,0:T(8,128)(2,1)}, u32[]{:S(2)}) copy-start(bf16[1,128,1024]{2,1,0:T(8,128)(2,1)} %param.13) | copy-start | bytes 786436
  21.0 305.1 %copy-start.3 = (s32[1,128]{1,0:T(1,128)S(1)}, s32[1,128]{1,0:T(1,128)}, u32[]{:S(2)}) copy-start(s32[1,128]{1,0:T(1,128)} %param.15) | copy-start | bytes 1540
  21.1 307.3 %all-to-all-start = ((bf16[16,1024,384]{1,2,0:T(8,128)(2,1)}), bf16[16,1024,384]{1,2,0:T(8,128)(2,1)}, u32[]{:S(2)}, u32[]{:S(2)}) async-start(bf16[16,1024,384]{1,2,0:T(8,128)(2,1)} %stack.3), calls=%async_computation | async-start | bytes 25165824 | tf_op jit(solution)/shard_map/all_to_all | solution.py:146
  28.8 299.3 %copy-start.2 = (f32[1,1024]{1,0:T(1,128)S(1)}, f32[1,1024]{1,0:T(1,128)}, u32[]{:S(2)}) copy-start(f32[1,1024]{1,0:T(1,128)} %param.16) | copy-start | bytes 12292
  28.8 362.8 %reduce-scatter.2.cloned.1.call-start = ((), (), s32[]{:S(2)}) async-start(), calls=%async_computation.2 | async-start | bytes 1769472 | tf_op jit(solution)/shard_map/reduce_scatter | solution.py:150
  391.7 5.9 %collective-permute-start = (bf16[128,768]{1,0:T(8,128)(2,1)}, bf16[128,768]{1,0:T(8,128)(2,1)S(1)}, u32[]{:S(2)}, u32[]{:S(2)}) collective-permute-start(bf16[128,768]{1,0:T(8,128)(2,1)} %reduce-scatter.2.cloned.1.call-done), channel_id=1, source_target_pairs={{0,1},{1,0},{2,3},{3,2},{4,5},{5,4},{6,7},{7,6},{8,9},{9,8},{10,11... | collective-permute-start | bytes 589832 | tf_op jit(solution)/shard_map/ppermute | solution.py:35
Sparse Core Ops, SparseCore 0:
  13.6 215.2 all-gather.3
  338.5 53.0 reduce-scatter.1
